TPU v7x, 256 devices: a whole 4x4x8 slice. The times are simulated.
256 devices in a mesh: row: 8 (over y, core), col: 32 (over z, x).
Axes of the slice: x: 4, y: 4, z: 8, core: 2. Of those that a mesh axis runs over, the one named last changes fastest.
Arguments:
- features: bfloat16 [4, 8, 32, 16, 512], P(None, 'row', 'col'), may hold values from -4 to 4, as said below
- left_factor: bfloat16 [4, 8, 512, 2, 32, 512], P(None, 'row', None, None, 'col'), as said below
- ard_weights: float32 [512], replicated, as said below
Outputs:
- panels: float32 [4, 8, 32, 16, 1024], P(None, 'row', 'col')
Inputs may be any that keep to these rules, and one draw needn't show every extreme that they name: `features`: independent entries of unit spread. `left_factor`: kernel minus left_update is positive definite on the first 1024 rows. `ard_weights`: independent positive entries between 0.005 and 0.18.
All inputs are finite; a program needn't handle non-finite values.
Results may differ from a plain program's by a relative error of at most 0.0003.
Values may be sent and summed in bfloat16 or wider, within the bound.
A program may use at most 64 MiB of HBM per device.

v0:
```python
import jax
import jax.numpy as jnp
from jax import lax
from jax.sharding import PartitionSpec as P


def from_root(x, axis, root):
    mine = lax.axis_index(axis) == root
    return lax.psum(jnp.where(mine, x, jnp.zeros_like(x)), axis)


def contract_rows(left_mat, right_mat):
    return lax.dot_general(
        left_mat,
        right_mat,
        (((1,), (1,)), ((), ())),
        precision=lax.Precision.HIGHEST,
        preferred_element_type=jnp.float32,
    )


def inverse_factor(matrix):
    factor = jnp.linalg.cholesky(matrix)
    identity_mat = jnp.eye(matrix.shape[0], dtype=jnp.float32)
    return jax.scipy.linalg.solve_triangular(factor, identity_mat, lower=True)


def kernel_block(rows_feat, panel_feat, ard_weights, row_ids, col_ids):
    scaled_rows = rows_feat.astype(jnp.float32) * ard_weights
    scaled_panel = panel_feat.astype(jnp.float32) * ard_weights
    sq_dist = (
        jnp.sum(scaled_rows * scaled_rows, axis=1)[:, None]
        + jnp.sum(scaled_panel * scaled_panel, axis=1)[None, :]
        - 2.0 * contract_rows(scaled_rows, scaled_panel)
    )
    jitter = jnp.where(row_ids[:, None] == col_ids[None, :], 0.01, 0.0).astype(jnp.float32)
    return jnp.exp(-0.5 * sq_dist) + jitter


def make_term(local_view, factor_rows, rows_here, num_rows):
    groups = num_rows // rows_here
    product_out = jnp.einsum(
        "imsk,pk->misp", local_view, factor_rows, preferred_element_type=jnp.float32
    )
    return product_out.reshape(groups * rows_here, factor_rows.shape[0])


def panel_update(local_view, factor_rows, rows_here):
    return lax.psum_scatter(
        make_term(local_view, factor_rows, rows_here, rows_here * lax.axis_size("col")),
        "col",
        scatter_dimension=0,
        tiled=True,
    )


def per_device(features, left_factor, ard_weights):
    row_blocks = features.shape[0]
    share_rows = features.shape[3]
    feat_width = features.shape[4]
    block_size = left_factor.shape[2]
    col_count = lax.axis_size("col")
    row_count = lax.axis_size("row")
    rows_here = row_blocks * share_rows
    local_view = left_factor.reshape(row_blocks, col_count, share_rows, -1)
    own_feats = features.reshape(rows_here, feat_width)
    block_feats = lax.all_gather(features[0, 0, 0], "col", axis=0, tiled=True)
    owners = []
    for panel_idx in range(2):
        owners.append(
            (
                from_root(local_view[0].reshape(block_size, -1), "row", panel_idx),
                from_root(block_feats, "row", panel_idx),
            )
        )
    panel_feats = jnp.concatenate([owners[0][1], owners[1][1]], axis=0)
    row_pos = lax.axis_index("row")
    col_pos = lax.axis_index("col")
    block_ids = jnp.arange(row_blocks, dtype=jnp.int32)[:, None] * row_count + row_pos
    row_ids = (
        block_ids * block_size
        + col_pos * share_rows
        + jnp.arange(share_rows, dtype=jnp.int32)[None, :]
    ).reshape(rows_here)
    col_ids = jnp.arange(2 * block_size, dtype=jnp.int32)
    kernel = kernel_block(own_feats, panel_feats, ard_weights, row_ids, col_ids)
    first_update = panel_update(local_view, owners[0][0], rows_here)
    second_update = panel_update(local_view, owners[1][0], rows_here)
    first_schur = kernel[:, :block_size] - first_update
    second_pre = kernel[:, block_size:] - second_update
    first_rows = lax.all_gather(first_schur[:share_rows], "col", axis=0, tiled=True)
    second_rows = lax.all_gather(second_pre[:share_rows], "col", axis=0, tiled=True)
    first_inv = inverse_factor(from_root(first_rows, "row", 0))
    first_panel = contract_rows(first_schur, first_inv)
    local_rows = contract_rows(first_rows, first_inv)
    local_diag = second_rows - contract_rows(local_rows, local_rows)
    lower_rows, lower_diag = (from_root(local_rows, "row", 1), from_root(local_diag, "row", 1))
    second_schur = second_pre - contract_rows(first_panel, lower_rows)
    second_inv = inverse_factor(lower_diag)
    second_panel = contract_rows(second_schur, second_inv)
    panels = jnp.concatenate([first_panel, second_panel], axis=1)
    return panels.reshape(row_blocks, 1, 1, share_rows, 2 * block_size)


def solution(mesh):
    return jax.shard_map(
        per_device,
        mesh=mesh,
        in_specs=(P(None, "row", "col", None, None), P(None, "row", None, None, "col", None), P()),
        out_specs=P(None, "row", "col", None, None),
        check_vma=False,
    )
```

profile of v0, /device:TPU:24, one launch (start us, length us, event | category | flops | bytes accessed | tf_op | source)
XLA Modules:
  0.0 1188.4 jit_solution(10306275246447917142)
XLA Ops:
  11.7 52.5 %all-gather = bf16[1,1,1,512,512]{4,3,2,1,0:T(8,128)(2,1)S(1)} all-gather(bf16[1,1,1,16,512]{4,3,2,1,0:T(8,128)(2,1)S(1)} %slice-done), channel_id=2, replica_groups=mesh['row'=8,'col'=32] {'col'}, dimensions={3}, use_global_device_ids=true | all-gather | bytes 540672 | tf_op jit(solution)/shard_map/all_gather | solution.py:67
  65.4 7.7 reshape.91
  73.1 61.7 %all-reduce.11.cloned.1.call-done = (bf16[512,1024]{1,0:T(8,128)(2,1)}, bf16[512,512]{1,0:T(8,128)(2,1)}, bf16[512,512]{1,0:T(8,128)(2,1)}, bf16[512,1024]{1,0:T(8,128)(2,1)}) async-done(((bf16[512,1024]{1,0:T(8,128)(2,1)}, bf16[512,512]{1,0:T(8,128)(2,1)}, bf16[512,512]{1,0:T(8,128)(2,1)}, bf16[512,1024]{1,0:T(8,128)(2,1)}), (bf16[512,1024]{1,0:T(8,128)(2,1)}, bf16[512,512]{1,0:T(8,128)(2,1)}, ...) | async-done | bytes 3145744 | tf_op jit(solution)/shard_map/psum | solution.py:9
  134.8 6.2 fusion.7
  141.0 4.4 copy.33
  146.6 5.8 fusion.4
  152.4 4.4 copy.27
  160.5 208.7 %reduce-scatter.9.cloned.1.call-done = f32[64,512]{1,0:T(8,128)} async-done(((f32[2048,512]{1,0:T(8,128)}), f32[64,512]{1,0:T(8,128)}) %reduce-scatter.9.cloned.1.call-update) | async-done | bytes 131088 | tf_op jit(solution)/shard_map/reduce_scatter | solution.py:49
  369.2 223.4 %reduce-scatter.7.cloned.1.call-done = f32[64,512]{1,0:T(8,128)} async-done(((f32[2048,512]{1,0:T(8,128)}), f32[64,512]{1,0:T(8,128)}) %reduce-scatter.7.cloned.1.call-update) | async-done | bytes 131088 | tf_op jit(solution)/shard_map/reduce_scatter | solution.py:49
  595.0 74.2 %all-gather.4.cloned.1.call-done = f32[512,512]{1,0:T(8,128)} async-done(((f32[16,512]{1,0:T(8,128)}), f32[512,512]{1,0:T(8,128)}) %all-gather.4.cloned.1.call-update) | async-done | bytes 1048592 | tf_op jit(solution)/shard_map/all_gather | solution.py:91
  672.3 73.2 %all-gather.6.cloned.1.call-done = f32[512,512]{1,0:T(8,128)} async-done(((f32[16,512]{1,0:T(8,128)}), f32[512,512]{1,0:T(8,128)}) %all-gather.6.cloned.1.call-update) | async-done | bytes 1048592 | tf_op jit(solution)/shard_map/all_gather | solution.py:92
  748.1 62.6 %all-reduce.7.cloned.1.call-done = f32[512,512]{0,1:T(8,128)} async-done(((f32[512,512]{0,1:T(8,128)}), f32[512,512]{0,1:T(8,128)}) %all-reduce.7.cloned.1.call-update) | async-done | bytes 1048592 | tf_op jit(solution)/shard_map/psum | solution.py:9
  813.8 11.7 cholesky.286
  825.7 9.8 custom-call.27
  836.8 12.5 %cholesky.305 = f32[128,128]{1,0:T(8,128)S(1)} custom-call(f32[128,128]{1,0:T(8,128)} %cholesky.430), custom_call_target="Cholesky" | custom-call | tf_op jit(solution)/shard_map/jit(cholesky)/cholesky | solution.py:23
  850.0 11.1 custom-call.28
  861.7 11.7 cholesky.326
  874.1 9.8 custom-call.29
  884.5 11.9 cholesky.343
  901.4 11.2 while.4
  912.6 39.3 %custom-call.30 = f32[4,128,128]{1,2,0:T(8,128)S(1)} custom-call(f32[4,128,128]{2,1,0:T(8,128)S(1)} %get-tuple-element.21), custom_call_target="InvertDiagBlocksLowerTriangular" | custom-call | tf_op jit(solution)/shard_map/jit(_solve_triangular)/triangular_solve | solution.py:25
  960.9 4.1 fusion.11
  968.3 68.1 %all-reduce.9.cloned.1.call-done = (f32[512,512]{0,1:T(8,128)}, f32[512,512]{0,1:T(8,128)}) async-done(((f32[512,512]{0,1:T(8,128)}, f32[512,512]{0,1:T(8,128)}), (f32[512,512]{0,1:T(8,128)}, f32[512,512]{0,1:T(8,128)})) %all-reduce.9.cloned.1.call-update) | async-done | bytes 2097168 | tf_op jit(solution)/shard_map/psum | solution.py:9
  1039.4 11.7 cholesky.358
  1051.7 9.8 custom-call.31
  1062.2 12.3 %cholesky.377 = f32[128,128]{1,0:T(8,128)} custom-call(f32[128,128]{1,0:T(8,128)S(1)} %cholesky.443), custom_call_target="Cholesky" | custom-call | tf_op jit(solution)/shard_map/jit(cholesky)/cholesky | solution.py:23
  1076.7 10.4 custom-call.32
  1088.6 11.8 cholesky.398
  1101.2 9.8 custom-call.33
  1111.6 11.7 cholesky.415
  1126.7 8.1 while.5
  1134.9 39.5 %custom-call.34 = f32[4,128,128]{1,2,0:T(8,128)S(1)} custom-call(f32[4,128,128]{2,1,0:T(8,128)S(1)} %get-tuple-element.22), custom_call_target="InvertDiagBlocksLowerTriangular" | custom-call | tf_op jit(solution)/shard_map/jit(_solve_triangular)/triangular_solve | solution.py:25
  (155 shorter events, 76.9 us)
Async XLA Ops:
  6.5 5.2 slice-start
  6.5 128.2 %all-reduce.11.cloned.1.call-start = ((), (), s32[]{:S(2)}) async-start(), calls=%async_computation.8 | async-start | bytes 6291456 | tf_op jit(solution)/shard_map/psum | solution.py:9
  65.3 303.9 %reduce-scatter.9.cloned.1.call-start = ((), (), s32[]{:S(2)}) async-start(), calls=%async_computation.6 | async-start | bytes 4325376 | tf_op jit(solution)/shard_map/reduce_scatter | solution.py:49
  145.4 1.2 copy-start.14
  145.4 447.2 %reduce-scatter.7.cloned.1.call-start = ((), (), s32[]{:S(2)}) async-start(), calls=%async_computation.5 | async-start | bytes 4325376 | tf_op jit(solution)/shard_map/reduce_scatter | solution.py:49
  156.8 0.8 copy-start.10
  156.8 0.8 copy-start.13
  156.8 1.1 copy-start.7
  156.8 1.2 copy-start.8
  156.8 512.5 %all-gather.4.cloned.1.call-start = ((), (), s32[]{:S(2)}) async-start(), calls=%async_computation.2 | async-start | bytes 1081344 | tf_op jit(solution)/shard_map/all_gather | solution.py:91
  593.6 154.5 %copy-start.11 = (f32[64,512]{1,0:T(8,128)}, f32[64,512]{1,0:T(8,128)S(1)}, u32[]{:S(2)}) copy-start(f32[64,512]{1,0:T(8,128)S(1)} %get-tuple-element.53) | copy-start | bytes 393220
  594.3 151.2 %all-gather.6.cloned.1.call-start = ((), (), s32[]{:S(2)}) async-start(), calls=%async_computation.4 | async-start | bytes 1081344 | tf_op jit(solution)/shard_map/all_gather | solution.py:92
  595.0 215.8 %all-reduce.7.cloned.1.call-start = ((), (), s32[]{:S(2)}) async-start(), calls=%async_computation.3 | async-start | bytes 2097152 | tf_op jit(solution)/shard_map/psum | solution.py:9
  671.9 364.4 %all-reduce.9.cloned.1.call-start = ((), (), s32[]{:S(2)}) async-start(), calls=%async_computation.7 | async-start | bytes 4194304 | tf_op jit(solution)/shard_map/psum | solution.py:9
  900.3 58.4 %copy-start = (f32[512,512]{1,0:T(8,128)S(1)}, f32[512,512]{1,0:T(8,128)}, u32[]{:S(2)}) copy-start(f32[512,512]{1,0:T(8,128)} %all-gather.4.cloned.1.call-done) | copy-start | bytes 3145732
  954.0 4.0 copy-start.1
  955.8 2.1 copy-start.3
  957.9 0.7 copy-start.5
  965.0 1.1 copy-start.2
  965.0 1.1 copy-start.4
  965.0 1.4 copy-start.6
  965.0 1.5 copy-start.12
  1126.5 51.0 %copy-start.9 = (f32[64,512]{1,0:T(8,128)S(1)}, f32[64,512]{1,0:T(8,128)}, u32[]{:S(2)}) copy-start(f32[64,512]{1,0:T(8,128)} %fusion.42) | copy-start | bytes 393220
Sparse Core Ops, SparseCore 0:
  65.4 69.2 all-reduce.10
  145.5 223.6 reduce-scatter.8
  373.6 218.9 reduce-scatter.6
  595.1 74.1 all-gather.3
  671.7 73.7 all-gather.5
  747.8 62.9 all-reduce.6
  966.2 70.1 all-reduce.8
where the time goes:
time: 1200 us; the launch traced here: 1190 us
  waiting for transfers between devices  772 us (64%)
  other arithmetic  254 us (21%)
  blocking collectives  52.5 us (4%)
  local copies, waits for them, and re-layouts  51.4 us (4%)
  matrix products  38.6 us (3%)
  between operations  19.3 us (2%)
    reduce_scatter x2, waiting for transfers between devices, panel_update(): lax.psum_scatter(make_term(local_view, factor_rows, rows_here, rows_here...  432 us
    psum x3, waiting for transfers between devices, from_root(): return lax.psum(jnp.where(mine, x, jnp.zeros_like(x)), axis)  192 us
    another operation x29, other arithmetic, inverse_factor(): factor = jnp.linalg.cholesky(matrix)  163 us
    another operation x5, other arithmetic, inverse_factor(): return jax.scipy.linalg.solve_triangular(factor, identity_mat, lower=True)  80.1 us
    all_gather x1, waiting for transfers between devices, per_device(): lax.all_gather(first_schur[:share_rows], 'col', axis=0, tiled=True)  74.2 us
    all_gather x1, waiting for transfers between devices, per_device(): lax.all_gather(second_pre[:share_rows], 'col', axis=0, tiled=True)  73.2 us
    all_gather x1, blocking collectives, per_device(): block_feats = lax.all_gather(features[0, 0, 0], 'col', axis=0, tiled=True)  52.5 us
  transfers between devices with their start and end apart: 7, of which 7 were waited for; matrix products, arithmetic and copies ran while one was open for 2% of the time, Pallas kernels for 0%

commit v1 on v0

v1 whole, which is shorter than its diff:
```python
import functools

import jax
import jax.numpy as jnp
from jax import lax
from jax.experimental import pallas as pl
from jax.experimental.pallas import tpu as pltpu
from jax.sharding import PartitionSpec as P

HIGHEST = lax.Precision.HIGHEST
MESH = pl.DeviceIdType.MESH
F32 = jnp.float32

NY, NX, NZ = 4, 4, 8
BLOCK = 512
PANELS = 2
SHARE = 16
LANES = 128
SPLITS = BLOCK // LANES
CHUNKS = 8
CHUNK_ROWS = BLOCK // CHUNKS
ROUNDS = ((0, 1), (1, 3))
HOPS = 6


def nt(left, right, precision=HIGHEST):
    return lax.dot_general(
        left, right, (((1,), (1,)), ((), ())), precision=precision, preferred_element_type=F32
    )


def sub_row(tile, j):
    return jnp.broadcast_to(tile[j : j + 1, :], (8, LANES))


def lane_col(tile, j):
    return jnp.broadcast_to(tile[:, j : j + 1], (8, LANES))


def diag_inverse(load_tile, store_tile):
    rows = lax.broadcasted_iota(jnp.int32, (8, LANES), 0)
    lanes = lax.broadcasted_iota(jnp.int32, (8, LANES), 1)
    tiles = LANES // 8
    a = [load_tile(v) for v in range(tiles)]
    e = [jnp.where(lanes == rows + 8 * v, 1.0, 0.0).astype(F32) for v in range(tiles)]
    for g in range(tiles):
        c = [lane_col(a[g], 8 * g + j) for j in range(8)]
        ta, tb, tf = a[g], e[g], e[g]
        scale = jnp.zeros((8, LANES), F32)
        for j in range(8):
            pivot = sub_row(c[j], j)
            recip = 1.0 / pivot
            scale = jnp.where(rows == j, lax.rsqrt(pivot), scale)
            cj = c[j]
            below = jnp.where(rows > j, cj, 0.0)

            def step(tile):
                unit = sub_row(tile, j) * recip
                return jnp.where(rows == j, unit, tile - cj * unit)

            for k in range(j + 1, 8):
                c[k] = step(c[k])
            if g < tiles - 1:
                ta, tb = step(ta), step(tb)
            tf = tf - below * (sub_row(tf, j) * recip)
        store_tile(g, tf * scale)
        if g < tiles - 1:
            wa = [sub_row(ta, j) for j in range(8)]
            wb = [sub_row(tb, j) for j in range(8)]
            for v in range(g + 1, tiles):
                m = [lane_col(a[v], 8 * g + j) for j in range(8)]

                def less(tile, w):
                    p = [m[j] * w[j] for j in range(8)]
                    return tile - (((p[0] + p[1]) + (p[2] + p[3])) + ((p[4] + p[5]) + (p[6] + p[7])))

                a[v] = less(a[v], wa)
                e[v] = less(e[v], wb)


def factor_kernel(s_ref, own_ref, out_ref, a, x, lp):
    n = s_ref.shape[0]
    a[:n, :] = s_ref[...]
    a[n:, :] = own_ref[...]

    def block(b, carry):
        off = pl.multiple_of(b * LANES, LANES)

        def load_tile(v):
            return a[pl.ds(pl.multiple_of(off + 8 * v, 8), 8), pl.ds(off, LANES)]

        def store_tile(g, tile):
            x[8 * g : 8 * g + 8, :] = tile

        diag_inverse(load_tile, store_tile)
        lp[...] = nt(a[:, pl.ds(off, LANES)], x[...])
        out_ref[:, pl.ds(off, LANES)] = lp[n:, :]

        def col(c, carry):
            coff = pl.multiple_of(c * LANES, LANES)
            a[:, pl.ds(coff, LANES)] -= nt(lp[...], lp[pl.ds(coff, LANES), :])
            return carry

        lax.fori_loop(b + 1, n // LANES, col, 0)
        return carry

    lax.fori_loop(0, n // LANES, block, 0)


def factor_panels(s_all, s_own):
    n, own = s_all.shape[0], s_own.shape[0]
    vmem = pl.BlockSpec(memory_space=pltpu.VMEM)
    return pl.pallas_call(
        factor_kernel,
        out_shape=jax.ShapeDtypeStruct((own, n), F32),
        in_specs=[vmem, vmem],
        out_specs=vmem,
        scratch_shapes=[
            pltpu.VMEM((n + own, n), F32),
            pltpu.VMEM((LANES, LANES), F32),
            pltpu.VMEM((n + own, LANES), F32),
        ],
        compiler_params=pltpu.CompilerParams(vmem_limit_bytes=48 * 2**20),
    )(s_all, s_own)


def ring_add(m, k, n):
    return lax.rem(m + (k + n), n)


def comm_kernel(
    lf, feats, wts, s_all, s_own,
    pan, fp, t, kern, bz1, bx1, bx2, bz2, sa, so,
    pan_s, pan_r, ft_s, ft_r, rs_s, rs_r, ag_s, ag_r, loc,
):
    row, col = lax.axis_index("row"), lax.axis_index("col")
    y, core = row // 2, lax.rem(row, 2)
    mz, mx = col // NX, lax.rem(col, NX)
    at_y0 = y == 0

    def dev(dy=0, dx=0, dz=0, other=False):
        yy, xx, zz = ring_add(y, dy, NY), ring_add(mx, dx, NX), ring_add(mz, dz, NZ)
        cc = 1 - core if other else core
        return (yy * 2 + cc, zz * NX + xx)

    yp, ym = dev(dy=1), dev(dy=-1)
    zp, zm = dev(dz=1), dev(dz=-1)
    xp, xm = dev(dx=1), dev(dx=-1)
    sib = dev(other=True)

    def rcopy(src, dst, ssem, rsem, target):
        return pltpu.make_async_remote_copy(
            src_ref=src, dst_ref=dst, send_sem=ssem, recv_sem=rsem,
            device_id=target, device_id_type=MESH,
        )

    barrier = pltpu.get_barrier_semaphore()
    for target in (yp, ym, zp, zm, xp, xm, sib):
        pl.semaphore_signal(barrier, inc=1, device_id=target, device_id_type=MESH)
    pl.semaphore_wait(barrier, 7)

    def gather_ops(n, m, slot, ssem, rsem, plus, minus, arrived=None):
        hp, hm = n // 2, n // 2 - 1

        def up(s):
            ref = slot(ring_add(m, -s, n))
            return rcopy(ref, ref, ssem(s), rsem(s), plus)

        def down(s):
            ref = slot(ring_add(m, s, n))
            return rcopy(ref, ref, ssem(hp + s), rsem(hp + s), minus)

        def start():
            up(0).start()
            down(0).start()
            if arrived is not None:
                arrived(m, 0)

        def step(s):
            k = ring_add(m, -1 - s, n)
            rcopy(slot(k), slot(k), ssem(s), rsem(s), plus).wait_recv()
            if s < hp - 1:
                up(s + 1).start()
            if arrived is not None:
                arrived(k, 1 + s)
            if s < hm:
                k = ring_add(m, 1 + s, n)
                rcopy(slot(k), slot(k), ssem(hp + s), rsem(hp + s), minus).wait_recv()
                if s < hm - 1:
                    down(s + 1).start()
                if arrived is not None:
                    arrived(k, 1 + hp + s)

        def drain():
            for s in range(hp):
                up(s).wait_send()
            for s in range(hm):
                down(s).wait_send()

        return start, step, drain

    def spread_ops(ref, ssem0, ssem1, rsem):
        def go():
            @pl.when(at_y0)
            def _():
                rcopy(ref, ref, ssem0, rsem, yp).start()
                rcopy(ref, ref, ssem1, rsem, ym).start()

            @pl.when(jnp.logical_not(at_y0))
            def _():
                rcopy(ref, ref, ssem0, rsem, yp).wait_recv()

            @pl.when(y == 1)
            def _():
                rcopy(ref, ref, ssem0, rsem, yp).start()

        def drain():
            @pl.when(y <= 1)
            def _():
                rcopy(ref, ref, ssem0, rsem, yp).wait_send()

            @pl.when(at_y0)
            def _():
                rcopy(ref, ref, ssem1, rsem, ym).wait_send()

        return go, drain

    pos = jnp.where(core == 0, y, ring_add(0, NY - y, NY))
    onward = (jnp.where(core == 0, yp[0], ym[0]), col)

    def pan_ref(b, c):
        return pan.at[b, pl.ds(c * CHUNK_ROWS, CHUNK_ROWS)]

    def ring_chunk(c):
        return rcopy(pan_ref(core, c), pan_ref(core, c), pan_s.at[0, c], pan_r.at[0, c], onward)

    def sib_chunk(c, b):
        return rcopy(pan_ref(b, c), pan_ref(b, c), pan_s.at[1, c], pan_r.at[1, c], sib)

    @pl.when(at_y0)
    def _():
        fp[core, mz, mx] = feats[0]
        own = pltpu.make_async_copy(lf.at[0], pan.at[core], loc.at[0])
        own.start()
        own.wait()

    f_spread, f_spread_drain = spread_ops(fp.at[core, mz, mx], ft_s.at[0], ft_s.at[1], ft_r.at[0])
    fx = gather_ops(NX, mx, lambda k: fp.at[core, mz, k], lambda i: ft_s.at[2 + i], lambda i: ft_r.at[2 + i], xp, xm)
    fz = gather_ops(NZ, mz, lambda k: fp.at[core, k], lambda i: ft_s.at[5 + i], lambda i: ft_r.at[5 + i], zp, zm)

    def f_sib(b):
        return rcopy(fp.at[b], fp.at[b], ft_s.at[12], ft_r.at[12], sib)

    def f_step(i):
        if i == 0:
            f_spread()
            fx[0]()
        elif i == 1:
            fx[1](0)
        elif i == 2:
            fx[1](1)
            fz[0]()
        elif i < 7:
            fz[1](i - 3)
        else:
            f_sib(core).start()

    def stream(b, h, rnd):
        i0, ni = ROUNDS[rnd]
        isl = pl.ds(i0, ni)
        q = b * SPLITS + h
        w = h // 2
        z_first = h % 2 == 0

        def part(axis, k):
            if z_first:
                return t.at[q, k, isl] if axis == "z" else t.at[q, mz, isl, k]
            return t.at[q, :, isl, k] if axis == "x" else t.at[q, k, isl, mx]

        def slot(axis, s):
            if z_first:
                return bz1.at[b, w, s, isl] if axis == "z" else bx2.at[b, w, s, isl]
            return bx1.at[b, w, s, :, isl] if axis == "x" else bz2.at[b, w, s, isl]

        order = ("z", "x") if z_first else ("x", "z")
        size = {"z": (NZ, mz, zp, zm), "x": (NX, mx, xp, xm)}
        base = {order[0]: 0, order[1]: size[order[0]][0] - 1}

        def copy(axis, src, s, target):
            i = base[axis] + s
            return rcopy(src, slot(axis, s), rs_s.at[rnd, q, i], rs_r.at[rnd, q, i], target)

        def begin(axis):
            n, m, plus, minus = size[axis]
            hp, hm = n // 2, n // 2 - 1
            copy(axis, part(axis, ring_add(m, hp, n)), 0, plus).start()
            copy(axis, part(axis, ring_add(m, -hm, n)), hp, minus).start()

        def hop(axis, s):
            n, m, plus, minus = size[axis]
            hp, hm = n // 2, n // 2 - 1
            here = slot(axis, s)
            copy(axis, here, s, plus).wait_recv()
            if s < hp - 1:
                here[...] = here[...] + part(axis, ring_add(m, hp - 1 - s, n))[...]
                copy(axis, here, s + 1, plus).start()
            if s < hm:
                there = slot(axis, hp + s)
                copy(axis, there, hp + s, minus).wait_recv()
                if s < hm - 1:
                    there[...] = there[...] + part(axis, ring_add(m, s + 1 - hm, n))[...]
                    copy(axis, there, hp + s + 1, minus).start()
            if s == hp - 1:
                mine = part(axis, m)
                mine[...] = mine[...] + (here[...] + slot(axis, hp + hm - 1)[...])
                if axis == order[0]:
                    begin(order[1])

        def macro(g):
            first = size[order[0]][0] // 2
            if g < first:
                hop(order[0], g)
            else:
                hop(order[1], g - first)

        def drain():
            for axis in order:
                n, m, plus, minus = size[axis]
                for s in range(n - 1):
                    copy(axis, slot(axis, s), s, plus).wait_send()

        return (lambda: begin(order[0])), macro, drain

    def rs_hop(rnd, g):
        for h in range(SPLITS):
            for b in range(PANELS):
                stream(b, h, rnd)[1](g)

    def product(b, h, i):
        rows = nt(lf[i], pan[b, h * LANES : (h + 1) * LANES, :], None)
        t[b * SPLITS + h, :, i] = rows.reshape(NZ, NX, SHARE, LANES)

    for c in range(CHUNKS):
        @pl.when(jnp.logical_not(at_y0))
        def _():
            ring_chunk(c).wait_recv()

        @pl.when(pos < NY - 1)
        def _():
            ring_chunk(c).start()

        sib_chunk(c, core).start()
        f_step(c)
        sib_chunk(c, 1 - core).wait_recv()
        if c % 2 == 1:
            for b in (core, 1 - core):
                product(b, c // 2, 0)
                stream(b, c // 2, 0)[0]()

    f_sib(1 - core).wait_recv()
    weights = wts[...]
    own_feat = feats[...].reshape(4 * SHARE, -1).astype(F32) * weights
    own_norm = jnp.sum(own_feat * own_feat, axis=1, keepdims=True)
    ids = lax.broadcasted_iota(jnp.int32, (4 * SHARE, BLOCK), 0)
    row_ids = ((ids // SHARE) * 8 + row) * BLOCK + col * SHARE + lax.rem(ids, SHARE)
    for b in range(PANELS):
        feat = fp[b].reshape(BLOCK, -1).astype(F32) * weights
        norm = nt(jnp.ones((8, feat.shape[1]), F32), feat * feat)[0:1, :]
        dist = own_norm + norm - 2.0 * nt(own_feat, feat)
        cols = lax.broadcasted_iota(jnp.int32, (4 * SHARE, BLOCK), 1) + b * BLOCK
        kern[:, b * BLOCK : (b + 1) * BLOCK] = jnp.exp(-0.5 * dist) + jnp.where(row_ids == cols, 0.01, 0.0).astype(F32)

    def rest(i, carry):
        for b in range(PANELS):
            for h in range(SPLITS):
                product(b, h, i)
        return carry

    lax.fori_loop(1, 4, rest, 0)

    rs_hop(0, 0)
    rs_hop(0, 1)
    for h in range(SPLITS):
        for b in range(PANELS):
            stream(b, h, 1)[0]()
    for g in range(2, HOPS):
        rs_hop(0, g)

    def schur(i):
        for q in range(PANELS * SPLITS):
            lanes = pl.ds(q * LANES, LANES)
            so[i, :, lanes] = kern[i * SHARE : (i + 1) * SHARE, lanes] - t[q, mz, i, mx]

    schur(0)

    left, right = pl.ds(0, BLOCK), pl.ds(BLOCK, BLOCK)
    sa[0, :, :, :, right] = jnp.zeros((NZ, NX, SHARE, BLOCK), F32)

    @pl.when(at_y0)
    def _():
        sa[core, mz, mx, :, left] = so[0, :, left]

        @pl.when(core == 1)
        def _():
            sa[1, mz, mx, :, right] = so[0, :, right]

    def to_sib(half, b, k, i):
        ref = sa.at[b, k, :, :, left] if half == 0 else sa.at[b, :, k, :, right]
        return rcopy(ref, ref, ag_s.at[half, 12 + i], ag_r.at[half, 12 + i], sib)

    def ag_sems(sems, half, base):
        return lambda i: sems.at[half, base + i]

    g0_spread, g0_spread_drain = spread_ops(sa.at[core, mz, mx, :, left], ag_s.at[0, 0], ag_s.at[0, 1], ag_r.at[0, 0])
    g0x = gather_ops(NX, mx, lambda k: sa.at[core, mz, k, :, left], ag_sems(ag_s, 0, 2), ag_sems(ag_r, 0, 2), xp, xm)
    g0z = gather_ops(NZ, mz, lambda k: sa.at[core, k, :, :, left], ag_sems(ag_s, 0, 5), ag_sems(ag_r, 0, 5), zp, zm,
                     lambda k, i: to_sib(0, core, k, i).start())
    g1_spread, g1_spread_drain = spread_ops(sa.at[1, mz, mx, :, right], ag_s.at[1, 0], ag_s.at[1, 1], ag_r.at[1, 0])
    g1z = gather_ops(NZ, mz, lambda k: sa.at[1, k, mx, :, right], ag_sems(ag_s, 1, 2), ag_sems(ag_r, 1, 2), zp, zm)
    g1x = gather_ops(NX, mx, lambda k: sa.at[1, :, k, :, right], ag_sems(ag_s, 1, 9), ag_sems(ag_r, 1, 9), xp, xm,
                     lambda k, i: to_sib(1, 1, k, i).start())

    def on_core1(fn):
        pl.when(core == 1)(fn)

    g0_spread()
    on_core1(g1_spread)
    g0x[0]()
    on_core1(g1z[0])
    g0x[1](0)
    g0x[1](1)
    g0z[0]()
    on_core1(lambda: g1z[1](0))
    on_core1(lambda: g1z[1](1))
    rs_hop(1, 0)
    g0z[1](0)
    g0z[1](1)

    def g1_mid():
        g1z[1](2)
        g1z[1](3)
        g1x[0]()

    on_core1(g1_mid)
    g0z[1](2)
    g0z[1](3)

    def g1_end():
        g1x[1](0)
        g1x[1](1)

    on_core1(g1_end)
    for i in range(NZ):
        k = ring_add(mz, (0, -1, -2, -3, -4, 1, 2, 3)[i], NZ)
        to_sib(0, 1 - core, k, i).wait_recv()

    @pl.when(core == 0)
    def _():
        for i in range(NX):
            k = ring_add(mx, (0, -1, -2, 1)[i], NX)
            to_sib(1, 1, k, i).wait_recv()

    for g in range(1, HOPS):
        rs_hop(1, g)
    for i in range(1, 4):
        schur(i)

    out_all = pltpu.make_async_copy(sa, s_all, loc.at[1])
    out_own = pltpu.make_async_copy(so, s_own, loc.at[2])
    out_all.start()
    out_own.start()

    @pl.when(pos < NY - 1)
    def _():
        for c in range(CHUNKS):
            ring_chunk(c).wait_send()

    for c in range(CHUNKS):
        sib_chunk(c, core).wait_send()
    f_spread_drain()
    fx[2]()
    fz[2]()
    f_sib(core).wait_send()
    for rnd in range(2):
        for b in range(PANELS):
            for h in range(SPLITS):
                stream(b, h, rnd)[2]()
    g0_spread_drain()
    g0x[2]()
    g0z[2]()
    for i in range(NZ):
        to_sib(0, core, 0, i).wait_send()

    def g1_drain():
        g1_spread_drain()
        g1z[2]()
        g1x[2]()
        for i in range(NX):
            to_sib(1, 1, 0, i).wait_send()

    on_core1(g1_drain)
    out_all.wait()
    out_own.wait()


def schur_rows(lf, feats, wts):
    vmem = pl.BlockSpec(memory_space=pltpu.VMEM)
    anyspace = pl.BlockSpec(memory_space=pl.ANY)
    width = lf.shape[2]
    fwidth = feats.shape[2]
    dma = pltpu.SemaphoreType.DMA
    return pl.pallas_call(
        comm_kernel,
        out_shape=(
            jax.ShapeDtypeStruct((PANELS, NZ, NX, SHARE, PANELS * BLOCK), F32),
            jax.ShapeDtypeStruct((4, SHARE, PANELS * BLOCK), F32),
        ),
        in_specs=[vmem, vmem, vmem],
        out_specs=(anyspace, anyspace),
        scratch_shapes=[
            pltpu.VMEM((PANELS, BLOCK, width), jnp.bfloat16),
            pltpu.VMEM((PANELS, NZ, NX, SHARE, fwidth), jnp.bfloat16),
            pltpu.VMEM((PANELS * SPLITS, NZ, 4, NX, SHARE, LANES), F32),
            pltpu.VMEM((4 * SHARE, PANELS * BLOCK), F32),
            pltpu.VMEM((PANELS, 2, NZ - 1, 4, NX, SHARE, LANES), F32),
            pltpu.VMEM((PANELS, 2, NX - 1, NZ, 4, SHARE, LANES), F32),
            pltpu.VMEM((PANELS, 2, NX - 1, 4, SHARE, LANES), F32),
            pltpu.VMEM((PANELS, 2, NZ - 1, 4, SHARE, LANES), F32),
            pltpu.VMEM((PANELS, NZ, NX, SHARE, PANELS * BLOCK), F32),
            pltpu.VMEM((4, SHARE, PANELS * BLOCK), F32),
            dma((2, CHUNKS)), dma((2, CHUNKS)),
            dma((13,)), dma((13,)),
            dma((2, PANELS * SPLITS, 10)), dma((2, PANELS * SPLITS, 10)),
            dma((2, 20)), dma((2, 20)),
            dma((3,)),
        ],
        compiler_params=pltpu.CompilerParams(
            collective_id=0, has_side_effects=True, vmem_limit_bytes=56 * 2**20
        ),
    )(lf, feats, wts)


def per_device(features, left_factor, ard_weights):
    lf = left_factor.reshape(4, BLOCK, -1)
    feats = features.reshape(4, SHARE, -1)
    s_all, s_own = schur_rows(lf, feats, ard_weights.reshape(1, -1))
    panels = factor_panels(s_all.reshape(PANELS * BLOCK, -1), s_own.reshape(4 * SHARE, -1))
    return panels.reshape(4, 1, 1, SHARE, PANELS * BLOCK)


def solution(mesh):
    return jax.shard_map(
        per_device,
        mesh=mesh,
        in_specs=(P(None, "row", "col", None, None), P(None, "row", None, None, "col", None), P()),
        out_specs=P(None, "row", "col", None, None),
        check_vma=False,
    )
```

time: 1200 us -> 271 us (0.23)
  waiting for transfers between devices: 772 us -> 0 us
  Pallas kernels: 0 us -> 260 us
  other arithmetic: 254 us -> 0 us
  blocking collectives: 52.5 us -> 0 us
  local copies, waits for them, and re-layouts: 51.4 us -> 10.8 us
  matrix products: 38.6 us -> 0 us
  between operations: 19.3 us -> 0.02 us
    reduce_scatter x2 -> x0, waiting for transfers between devices: 432 us -> none  [panel_update(): lax.psum_scatter(make_term(local_view, factor_rows, rows_here, rows_here...]
    pallas_call x0 -> x2, Pallas kernels: none -> 260 us  [the longest x1 199 us: schur_rows(): pl.pallas_call(comm_kernel, out_shape=(jax.ShapeDtypeStruct((PANELS, NZ,...]
    another operation x34 -> x0, other arithmetic: 243 us -> none  [the longest x29 163 us: inverse_factor(): factor = jnp.linalg.cholesky(matrix)]
    psum x3 -> x0, waiting for transfers between devices: 192 us -> none  [from_root(): return lax.psum(jnp.where(mine, x, jnp.zeros_like(x)), axis)]
    all_gather x2 -> x0, waiting for transfers between devices: 147 us -> none  [the longest x1 74.2 us: per_device(): lax.all_gather(first_schur[:share_rows], 'col', axis=0, tiled=True)]
    all_gather x1 -> x0, blocking collectives: 52.5 us -> none  [per_device(): block_feats = lax.all_gather(features[0, 0, 0], 'col', axis=0, tiled=True)]
    dot_general x8 -> x0, matrix products: 25 us -> none  [the longest x6 12.9 us: contract_rows(): lax.dot_general(left_mat, right_mat, (((1,), (1,)), ((), ())), precision=...]
    another operation x35 -> x0, local copies, waits for them, and re-layouts: 20.5 us -> none  [the longest x27 19.2 us: inverse_factor(): return jax.scipy.linalg.solve_triangular(factor, identity_mat, lower=True)]
  transfers between devices with their start and end apart: 7 -> 0, of which waited for: 7 -> 0; matrix products, arithmetic and copies ran while one was open for 2% -> 0% of each run, Pallas kernels for 0% -> 0%
where the time goes in v1:
time: 271 us; the launch traced here: 270 us
  Pallas kernels  260 us (96%)
  local copies, waits for them, and re-layouts  10.8 us (4%)
    pallas_call x1, Pallas kernels, schur_rows(): pl.pallas_call(comm_kernel, out_shape=(jax.ShapeDtypeStruct((PANELS, NZ,...  199 us
    pallas_call x1, Pallas kernels, factor_panels(): pl.pallas_call(factor_kernel, out_shape=jax.ShapeDtypeStruct((own, n), F3...  61 us
    reshape x1, local copies, waits for them, and re-layouts, per_device(): lf = left_factor.reshape(4, BLOCK, -1)  7.7 us

profile of v1, /device:TPU:24, one launch (start us, length us, event | category | flops | bytes accessed | tf_op | source)
XLA Modules:
  0.0 270.4 jit_solution(13600826327340181864)
XLA Ops:
  0.0 7.7 %reshape.18.lf = bf16[4,512,1024]{2,1,0:T(8,128)(2,1)} reshape(bf16[4,1,512,2,1,512]{5,3,4,2,1,0:T(2,128)(2,1)} %param.4) | data formatting | bytes 8388608 | tf_op jit(solution)/shard_map/reshape | solution.py:544
  7.7 198.5 %shard_map.37 = (f32[2,8,4,16,1024]{4,3,2,1,0:T(8,128)}, f32[4,16,1024]{2,1,0:T(8,128)}) custom-call(bf16[4,512,1024]{2,1,0:T(8,128)(2,1)} %reshape.18.lf, bf16[4,16,512]{2,1,0:T(8,128)(2,1)} %bitcast.11, f32[1,512]{1,0:T(1,128)} %bitcast.12), custom_call_target="tpu_custom_call" | custom-call | tf_op jit(solution)/shard_map/pallas_call | solution.py:512
  206.2 0.0 copy-start
  206.2 2.2 copy-done
  208.4 0.0 copy-start.1
  208.4 0.9 copy-done.1
  209.4 61.0 %shard_map.38 = f32[64,1024]{1,0:T(8,128)} custom-call(f32[1024,1024]{1,0:T(8,128)S(1)} %bitcast.9, f32[64,1024]{1,0:T(8,128)S(1)} %bitcast.10), custom_call_target="tpu_custom_call" | custom-call | tf_op jit(solution)/shard_map/pallas_call | solution.py:113
Async XLA Ops:
  206.2 2.2 copy-start
  208.4 0.9 copy-start.1

commit v2 on v0

v2 whole, which is shorter than its diff:
```python
import functools

import jax
import jax.numpy as jnp
from jax import lax
from jax.experimental import pallas as pl
from jax.experimental.pallas import tpu as pltpu
from jax.sharding import PartitionSpec as P

HIGHEST = lax.Precision.HIGHEST
MESH = pl.DeviceIdType.MESH
F32 = jnp.float32

NY, NX, NZ = 4, 4, 8
BLOCK = 512
PANELS = 2
SHARE = 16
LANES = 128
SPLITS = BLOCK // LANES
CHUNKS = 8
CHUNK_ROWS = BLOCK // CHUNKS
ROUNDS = ((0, 4), (1, 3))
HOPS = 6
BF16 = jnp.bfloat16


def nt(left, right, precision=HIGHEST):
    return lax.dot_general(
        left, right, (((1,), (1,)), ((), ())), precision=precision, preferred_element_type=F32
    )


def sub_row(tile, j):
    return jnp.broadcast_to(tile[j : j + 1, :], (8, LANES))


def lane_col(tile, j):
    return jnp.broadcast_to(tile[:, j : j + 1], (8, LANES))


def diag_inverse(load_tile, store_tile):
    rows = lax.broadcasted_iota(jnp.int32, (8, LANES), 0)
    lanes = lax.broadcasted_iota(jnp.int32, (8, LANES), 1)
    tiles = LANES // 8
    a = [load_tile(v) for v in range(tiles)]
    e = [jnp.where(lanes == rows + 8 * v, 1.0, 0.0).astype(F32) for v in range(tiles)]
    for g in range(tiles):
        c = [lane_col(a[g], 8 * g + j) for j in range(8)]
        ta, tb, tf = a[g], e[g], e[g]
        scale = jnp.zeros((8, LANES), F32)
        for j in range(8):
            pivot = sub_row(c[j], j)
            recip = 1.0 / pivot
            scale = jnp.where(rows == j, lax.rsqrt(pivot), scale)
            cj = c[j]
            below = jnp.where(rows > j, cj, 0.0)

            def step(tile):
                unit = sub_row(tile, j) * recip
                return jnp.where(rows == j, unit, tile - cj * unit)

            for k in range(j + 1, 8):
                c[k] = step(c[k])
            if g < tiles - 1:
                ta, tb = step(ta), step(tb)
            tf = tf - below * (sub_row(tf, j) * recip)
        store_tile(g, tf * scale)
        if g < tiles - 1:
            wa = [sub_row(ta, j) for j in range(8)]
            wb = [sub_row(tb, j) for j in range(8)]
            for v in range(g + 1, tiles):
                m = [lane_col(a[v], 8 * g + j) for j in range(8)]

                def less(tile, w):
                    p = [m[j] * w[j] for j in range(8)]
                    return tile - (((p[0] + p[1]) + (p[2] + p[3])) + ((p[4] + p[5]) + (p[6] + p[7])))

                a[v] = less(a[v], wa)
                e[v] = less(e[v], wb)


def halves(value):
    high = value.astype(BF16)
    return high, (value - high.astype(F32)).astype(BF16)


def nt_halves(left, right):
    return nt(left[0], right[0], None) + (nt(left[0], right[1], None) + nt(left[1], right[0], None))


def ring_add(m, k, n):
    return lax.rem(m + (k + n), n)


def panels_kernel(
    lf_in, feats, wts, out_ref,
    raw, rt, lf, pan, fp, t, kern, bz1, bx1, bx2, bz2, rx, rz, sa, own_s,
    lo, xs, col_buf, dg, po,
    pan_s, pan_r, ft_s, ft_r, rs_s, rs_r, dg_s, dg_r, loc,
):
    row, col = lax.axis_index("row"), lax.axis_index("col")
    y, core = row // 2, lax.rem(row, 2)
    mz, mx = col // NX, lax.rem(col, NX)
    at_y0 = y == 0
    off_y0 = jnp.logical_not(at_y0)
    n_cols = PANELS * BLOCK

    def dev(dy=0, dx=0, dz=0, other=False):
        yy, xx, zz = ring_add(y, dy, NY), ring_add(mx, dx, NX), ring_add(mz, dz, NZ)
        cc = 1 - core if other else core
        return (yy * 2 + cc, zz * NX + xx)

    yp, ym = dev(dy=1), dev(dy=-1)
    zp, zm = dev(dz=1), dev(dz=-1)
    xp, xm = dev(dx=1), dev(dx=-1)
    sib = dev(other=True)

    def rcopy(src, dst, ssem, rsem, target):
        return pltpu.make_async_remote_copy(
            src_ref=src, dst_ref=dst, send_sem=ssem, recv_sem=rsem,
            device_id=target, device_id_type=MESH,
        )

    raw_copies = [pltpu.make_async_copy(lf_in.at[i], raw.at[i], loc.at[i]) for i in range(4)]
    for copy in raw_copies:
        copy.start()
    barrier = pltpu.get_barrier_semaphore()
    peers = [dev(dz=k) for k in range(1, NZ)] + [dev(dx=k) for k in range(1, NX)]
    peers += [dev(dy=k) for k in range(1, NY)] + [sib]
    for target in peers:
        pl.semaphore_signal(barrier, inc=1, device_id=target, device_id_type=MESH)

    def relayout(i, c, stores):
        rows = pl.ds(c * CHUNK_ROWS, CHUNK_ROWS)
        value = raw[i, rows].astype(F32).reshape(2 * CHUNK_ROWS, BLOCK)
        for lane in range(SPLITS):
            rt[lane] = value[:, lane * LANES : (lane + 1) * LANES]
        for j in range(2):
            for lane in range(SPLITS):
                part = rt[lane, pl.ds(j, CHUNK_ROWS, stride=2), :].astype(BF16)
                lanes = pl.ds(j * BLOCK + lane * LANES, LANES)
                for store in stores:
                    store(rows, lanes, part)

    def to_lf(i):
        def store(rows, lanes, part):
            lf[i, rows, lanes] = part

        return store

    def to_pan(rows, lanes, part):
        pan[core, rows, lanes] = part

    def relayout_blocks(first):
        def go(k, carry):
            i, c = first + k // CHUNKS, lax.rem(k, CHUNKS)
            relayout(i, c, [to_lf(i)])
            return carry

        lax.fori_loop(0, (4 - first) * CHUNKS, go, 0)

    pos = jnp.where(core == 0, y, ring_add(0, NY - y, NY))
    onward = (jnp.where(core == 0, yp[0], ym[0]), col)

    def pan_ref(b, c):
        return pan.at[b, pl.ds(c * CHUNK_ROWS, CHUNK_ROWS)]

    def ring_chunk(c):
        return rcopy(pan_ref(core, c), pan_ref(core, c), pan_s.at[0, c], pan_r.at[0, c], onward)

    def sib_chunk(c, b):
        return rcopy(pan_ref(b, c), pan_ref(b, c), pan_s.at[1, c], pan_r.at[1, c], sib)

    def f_slab():
        return fp.at[core, mz, mx]

    def f_y(k):
        return rcopy(f_slab(), f_slab(), ft_s.at[k - 1], ft_r.at[0], dev(dy=k))

    def f_z(k, z):
        ref = fp.at[core, z, mx]
        return rcopy(ref, ref, ft_s.at[2 + k], ft_r.at[2 + k], dev(dz=k))

    def f_x(k, x):
        ref = fp.at[core, :, x]
        return rcopy(ref, ref, ft_s.at[9 + k], ft_r.at[9 + k], dev(dx=k))

    def f_sib(b):
        return rcopy(fp.at[b], fp.at[b], ft_s.at[13], ft_r.at[13], sib)

    def f_z_start():
        for k in range(1, NZ):
            f_z(k, mz).start()

    def f_x_start():
        for k in range(1, NZ):
            f_z(k, ring_add(mz, -k, NZ)).wait_recv()
        for k in range(1, NX):
            f_x(k, mx).start()

    def f_sib_start():
        for k in range(1, NX):
            f_x(k, ring_add(mx, -k, NX)).wait_recv()
        f_sib(core).start()

    def stream(b, h, rnd):
        i0, ni = ROUNDS[rnd]
        isl = pl.ds(i0, ni)
        q = b * SPLITS + h
        w = h // 2
        z_first = h % 2 == 0
        sign = 1 if w == 0 else -1

        def part(axis, k):
            if z_first:
                return t.at[q, k, isl] if axis == "z" else t.at[q, mz, isl, k]
            return t.at[q, :, isl, k] if axis == "x" else t.at[q, k, isl, mx]

        def slot(axis, s):
            if z_first:
                return bz1.at[b, w, s, isl] if axis == "z" else bx2.at[b, w, s, isl]
            return bx1.at[b, w, s, :, isl] if axis == "x" else bz2.at[b, w, s, isl]

        order = ("z", "x") if z_first else ("x", "z")
        size = {
            "z": (NZ, mz) + ((zp, zm) if sign > 0 else (zm, zp)),
            "x": (NX, mx) + ((xp, xm) if sign > 0 else (xm, xp)),
        }
        base = {order[0]: 0, order[1]: size[order[0]][0] - 1}

        def copy(axis, src, s, target):
            i = base[axis] + s
            return rcopy(src, slot(axis, s), rs_s.at[q, i], rs_r.at[q, i], target)

        def begin(axis):
            n, m, plus, minus = size[axis]
            hp, hm = n // 2, n // 2 - 1
            copy(axis, part(axis, ring_add(m, sign * hp, n)), 0, plus).start()
            copy(axis, part(axis, ring_add(m, -sign * hm, n)), hp, minus).start()

        def hop(axis, s):
            n, m, plus, minus = size[axis]
            hp, hm = n // 2, n // 2 - 1
            here = slot(axis, s)
            copy(axis, here, s, plus).wait_recv()
            if s < hp - 1:
                here[...] = here[...] + part(axis, ring_add(m, sign * (hp - 1 - s), n))[...]
                copy(axis, here, s + 1, plus).start()
            if s < hm:
                there = slot(axis, hp + s)
                copy(axis, there, hp + s, minus).wait_recv()
                if s < hm - 1:
                    there[...] = there[...] + part(axis, ring_add(m, sign * (s + 1 - hm), n))[...]
                    copy(axis, there, hp + s + 1, minus).start()
            if s == hp - 1:
                mine = part(axis, m)
                mine[...] = mine[...] + (here[...] + slot(axis, hp + hm - 1)[...])
                if axis == order[0]:
                    begin(order[1])

        def macro(g):
            first = size[order[0]][0] // 2
            if g < first:
                hop(order[0], g)
            else:
                hop(order[1], g - first)

        def drain():
            for axis in order:
                n, m, plus, minus = size[axis]
                for s in range(n - 1):
                    copy(axis, slot(axis, s), s, plus).wait_send()

        return (lambda: begin(order[0])), macro, drain

    def rs_hop(g):
        def go(rnd):
            for h in range(SPLITS):
                for b in range(PANELS):
                    stream(b, h, rnd)[1](g)

        pl.when(off_y0)(lambda: go(0))
        pl.when(at_y0)(lambda: go(1))

    def product(b, h, i):
        rows = nt(lf[i], pan[b, h * LANES : (h + 1) * LANES, :], None)
        t[b * SPLITS + h, :, i] = rows.reshape(NZ, NX, SHARE, LANES)

    def lanes_of(j):
        return pl.ds(j * LANES, LANES)

    def dcopy(src, dst, j, i, target):
        return rcopy(src, dst, dg_s.at[j, i], dg_r.at[j, i], target)

    def rsx(j, k):
        return dcopy(t.at[j, :, 0, ring_add(mx, k, NX)], rx.at[j, k - 1], j, k - 1, dev(dx=k))

    def rsz(j, k):
        return dcopy(t.at[j, ring_add(mz, k, NZ), 0, mx], rz.at[j, k - 1], j, 2 + k, dev(dz=k))

    def agy(j, k):
        ref = sa.at[core, mz, mx, :, lanes_of(j)]
        return rcopy(ref, ref, dg_s.at[j, 9 + k], dg_r.at[j, 10], dev(dy=k))

    def agz(j, k, z):
        ref = sa.at[core, z, mx, :, lanes_of(j)]
        return dcopy(ref, ref, j, 12 + k, dev(dz=k))

    def agx(j, k, x):
        ref = sa.at[core, :, x, :, lanes_of(j)]
        return dcopy(ref, ref, j, 19 + k, dev(dx=k))

    def ags(j, k, b):
        ref = sa.at[b, :, ring_add(mx, -k, NX), :, lanes_of(j)]
        return dcopy(ref, ref, j, 23 + k, sib)

    def gathers(j, fn):
        if j < SPLITS:
            fn()
        else:
            pl.when(core == 1)(fn)

    def rsx_start(j):
        for k in range(1, NX):
            rsx(j, k).start()

    def rsx_done(j):
        for k in range(1, NX):
            rsx(j, k).wait_recv()
        total = t[j, :, 0, mx] + rx[j, 0]
        t[j, :, 0, mx] = total + (rx[j, 1] + rx[j, 2])
        for k in range(1, NZ):
            rsz(j, k).start()

    def rsz_done(j):
        for k in range(1, NZ):
            rsz(j, k).wait_recv()
        total = t[j, mz, 0, mx] + rz[j, 0]
        for k in range(1, NZ - 1, 2):
            total = total + (rz[j, k] + rz[j, k + 1])
        lanes = lanes_of(j)
        schur = kern[0:SHARE, lanes] - total
        own_s[0:SHARE, lanes] = schur

        def send():
            sa[core, mz, mx, :, lanes] = schur
            for k in range(1, NY):
                agy(j, k).start()
            for k in range(1, NZ):
                agz(j, k, mz).start()

        gathers(j, send)

    def agy_done(j):
        def go():
            agy(j, 1).wait_recv()
            for k in range(1, NZ):
                agz(j, k, mz).start()

        gathers(j, go)

    def agz_done(j):
        def go():
            for k in range(1, NZ):
                agz(j, k, ring_add(mz, -k, NZ)).wait_recv()
            for k in range(1, NX):
                agx(j, k, mx).start()
            ags(j, 0, core).start()

        gathers(j, go)

    def agx_done(j):
        def go():
            for k in range(1, NX):
                agx(j, k, ring_add(mx, -k, NX)).wait_recv()
                ags(j, k, core).start()

        gathers(j, go)

    def sib_done(j):
        def go():
            for k in range(NX):
                ags(j, k, 1 - core).wait_recv()

        if j < SPLITS:
            go()
        else:
            pl.when(core == 0)(go)

    def own_kernel():
        weights = wts[...]
        own_feat = feats[...].reshape(4 * SHARE, -1).astype(F32) * weights
        own_norm = jnp.sum(own_feat * own_feat, axis=1, keepdims=True)
        ids = lax.broadcasted_iota(jnp.int32, (4 * SHARE, BLOCK), 0)
        row_ids = ((ids // SHARE) * 8 + row) * BLOCK + col * SHARE + lax.rem(ids, SHARE)
        for b in range(PANELS):
            feat = fp[b].reshape(BLOCK, -1).astype(F32) * weights
            norm = nt(jnp.ones((8, feat.shape[1]), F32), feat * feat)[0:1, :]
            dist = own_norm + norm - 2.0 * nt(own_feat, feat)
            cols = lax.broadcasted_iota(jnp.int32, (4 * SHARE, BLOCK), 1) + b * BLOCK
            jitter = jnp.where(row_ids == cols, 0.01, 0.0).astype(F32)
            kern[:, b * BLOCK : (b + 1) * BLOCK] = jnp.exp(-0.5 * dist) + jitter

    @pl.when(at_y0)
    def _():
        fp[core, mz, mx] = feats[0]

    raw_copies[0].wait()
    pl.semaphore_wait(barrier, len(peers))

    @pl.when(at_y0)
    def _():
        for k in range(1, NY):
            f_y(k).start()
        f_z_start()
        for c in range(CHUNKS):
            relayout(0, c, [to_lf(0), to_pan])
            sib_chunk(c, core).start()
            ring_chunk(c).start()

    lo[...] = jnp.zeros(lo.shape, BF16)
    po[...] = jnp.zeros(po.shape, BF16)
    sa[0, :, :, :, pl.ds(BLOCK, BLOCK)] = jnp.zeros((NZ, NX, SHARE, BLOCK), F32)
    for copy in raw_copies[1:]:
        copy.wait()

    @pl.when(at_y0)
    def _():
        for h in range(SPLITS):
            sib_chunk(2 * h, 1 - core).wait_recv()
            sib_chunk(2 * h + 1, 1 - core).wait_recv()
            product(0, h, 0)
            rsx_start(h)
        f_x_start()
        relayout_blocks(1)

        def rest(b):
            def go(i, carry):
                for h in range(SPLITS):
                    product(b, h, i)
                return carry

            lax.fori_loop(1, 4, go, 0)
            for h in range(SPLITS):
                stream(b, h, 1)[0]()

        rest(0)
        for j in range(SPLITS):
            rsx_done(j)
        f_sib_start()
        for h in range(SPLITS):
            product(1, h, 0)
            rsx_start(SPLITS + h)
        f_sib(1 - core).wait_recv()
        own_kernel()
        for j in range(SPLITS):
            rsz_done(j)
        rest(1)
        for j in range(SPLITS, 2 * SPLITS):
            rsx_done(j)

    @pl.when(off_y0)
    def _():
        relayout_blocks(0)
        f_y(1).wait_recv()
        f_z_start()
        for c in range(CHUNKS):
            ring_chunk(c).wait_recv()

            @pl.when(pos < NY - 1)
            def _():
                ring_chunk(c).start()

            sib_chunk(c, core).start()
            sib_chunk(c, 1 - core).wait_recv()
            if c == 3:
                f_x_start()
            if c % 2 == 1:
                def go(i, carry):
                    product(0, c // 2, i)
                    product(1, c // 2, i)
                    return carry

                lax.fori_loop(0, 4, go, 0)
                for b in range(PANELS):
                    stream(b, c // 2, 0)[0]()
        f_sib_start()
        f_sib(1 - core).wait_recv()
        own_kernel()
        for j in range(SPLITS):
            agy_done(j)

    def store_inverse(b):
        def store(g, tile):
            xs[b, 8 * g : 8 * g + 8, :] = tile

        return store

    def block_of(value):
        return lambda v: value[8 * v : 8 * v + 8, :]

    def rest_of(b):
        off = pl.multiple_of(b * LANES, LANES)
        noff = pl.multiple_of(off + LANES, LANES)
        for i, half in enumerate(halves(nt(col_buf[lax.rem(b, 2)], xs[b]))):
            lo[i, :, pl.ds(off, LANES)] = half
        update = nt_halves((lo[0], lo[1]), (lo[0, pl.ds(noff, LANES), :], lo[1, pl.ds(noff, LANES), :]))
        col_buf[lax.rem(b + 1, 2)] = sa[:, :, :, :, pl.ds(noff, LANES)].reshape(n_cols, LANES) - update

    def next_diag(b):
        off = pl.multiple_of(b * LANES, LANES)
        noff = pl.multiple_of(off + LANES, LANES)
        below = halves(nt(col_buf[lax.rem(b, 2), pl.ds(noff, LANES), :], xs[b]))
        b1 = b + 1
        block = sa[b1 // SPLITS, pl.ds(2 * lax.rem(b1, SPLITS), 2), :, :, pl.ds(noff, LANES)]
        done = (lo[0, pl.ds(noff, LANES), :], lo[1, pl.ds(noff, LANES), :])
        dg[...] = block.reshape(LANES, LANES) - nt_halves(done, done) - nt_halves(below, below)
        diag_inverse(block_of(dg[...]), store_inverse(b1))

    def own_rows(b):
        lanes = pl.ds(pl.multiple_of(b * LANES, LANES), LANES)
        found = nt_halves((po[0], po[1]), (lo[0, lanes, :], lo[1, lanes, :]))
        panel = nt(own_s[:, lanes] - found, xs[b])
        out_ref[:, lanes] = panel
        for i, half in enumerate(halves(panel)):
            po[i, :, lanes] = half

    second = range(SPLITS, 2 * SPLITS)
    agz_done(0)
    agz_done(1)
    agx_done(0)
    agz_done(2)
    agx_done(1)
    sib_done(0)
    col_buf[0] = sa[:, :, :, :, pl.ds(0, LANES)].reshape(n_cols, LANES)
    diag_inverse(block_of(col_buf[0, 0:LANES, :]), store_inverse(0))

    def before_0():
        @pl.when(at_y0)
        def _():
            for j in second:
                rsz_done(j)

        agz_done(3)
        agx_done(2)
        sib_done(1)

    def before_1():
        @pl.when(off_y0)
        def _():
            for j in second:
                agy_done(j)

        agx_done(3)
        sib_done(2)
        rs_hop(0)

    def before_2():
        for j in second:
            agz_done(j)
        sib_done(3)
        rs_hop(1)

    def before_3():
        for j in second:
            agx_done(j)
        sib_done(4)
        rs_hop(2)

    def before_4():
        sib_done(5)
        rs_hop(3)

    def before_5():
        sib_done(6)
        rs_hop(4)

    def step(b, carry):
        for k, fn in enumerate((before_0, before_1, before_2, before_3, before_4, before_5)):
            pl.when(b == k)(fn)
        next_diag(b)
        rest_of(b)
        return carry

    lax.fori_loop(0, 6, step, 0)
    sib_done(7)
    rs_hop(5)

    def own_schur(i):
        for q in range(PANELS * SPLITS):
            lanes = lanes_of(q)
            own_s[i * SHARE : (i + 1) * SHARE, lanes] = kern[i * SHARE : (i + 1) * SHARE, lanes] - t[q, mz, i, mx]

    pl.when(off_y0)(lambda: own_schur(0))
    for i in range(1, 4):
        own_schur(i)
    next_diag(6)
    rest_of(6)
    for b in range(8):
        own_rows(b)

    @pl.when(pos < NY - 1)
    def _():
        for c in range(CHUNKS):
            ring_chunk(c).wait_send()

    for c in range(CHUNKS):
        sib_chunk(c, core).wait_send()

    @pl.when(at_y0)
    def _():
        for k in range(1, NY):
            f_y(k).wait_send()

    for k in range(1, NZ):
        f_z(k, mz).wait_send()
    for k in range(1, NX):
        f_x(k, mx).wait_send()
    f_sib(core).wait_send()

    def drain_streams(rnd):
        for b in range(PANELS):
            for h in range(SPLITS):
                stream(b, h, rnd)[2]()

    pl.when(off_y0)(lambda: drain_streams(0))
    pl.when(at_y0)(lambda: drain_streams(1))
    for j in range(2 * SPLITS):
        @pl.when(at_y0)
        def _():
            for k in range(1, NX):
                rsx(j, k).wait_send()
            for k in range(1, NZ):
                rsz(j, k).wait_send()

            def sent():
                for k in range(1, NY):
                    agy(j, k).wait_send()

            gathers(j, sent)

        def sent_all():
            for k in range(1, NZ):
                agz(j, k, mz).wait_send()
            for k in range(1, NX):
                agx(j, k, mx).wait_send()
            for k in range(NX):
                ags(j, k, core).wait_send()

        gathers(j, sent_all)


def panels_of(lf, feats, wts):
    vmem = pl.BlockSpec(memory_space=pltpu.VMEM)
    anyspace = pl.BlockSpec(memory_space=pl.ANY)
    width = lf.shape[2] * lf.shape[3]
    fwidth = feats.shape[2]
    own, n = 4 * SHARE, PANELS * BLOCK
    dma = pltpu.SemaphoreType.DMA
    return pl.pallas_call(
        panels_kernel,
        out_shape=jax.ShapeDtypeStruct((own, n), F32),
        in_specs=[anyspace, vmem, vmem],
        out_specs=vmem,
        scratch_shapes=[
            pltpu.VMEM(lf.shape, BF16),
            pltpu.VMEM((SPLITS, 2 * CHUNK_ROWS, LANES), F32),
            pltpu.VMEM((4, BLOCK, width), BF16),
            pltpu.VMEM((PANELS, BLOCK, width), BF16),
            pltpu.VMEM((PANELS, NZ, NX, SHARE, fwidth), BF16),
            pltpu.VMEM((PANELS * SPLITS, NZ, 4, NX, SHARE, LANES), F32),
            pltpu.VMEM((own, n), F32),
            pltpu.VMEM((PANELS, 2, NZ - 1, 4, NX, SHARE, LANES), F32),
            pltpu.VMEM((PANELS, 2, NX - 1, NZ, 4, SHARE, LANES), F32),
            pltpu.VMEM((PANELS, 2, NX - 1, 4, SHARE, LANES), F32),
            pltpu.VMEM((PANELS, 2, NZ - 1, 4, SHARE, LANES), F32),
            pltpu.VMEM((PANELS * SPLITS, NX - 1, NZ, SHARE, LANES), F32),
            pltpu.VMEM((PANELS * SPLITS, NZ - 1, SHARE, LANES), F32),
            pltpu.VMEM((PANELS, NZ, NX, SHARE, n), F32),
            pltpu.VMEM((own, n), F32),
            pltpu.VMEM((2, n, n), BF16),
            pltpu.VMEM((n // LANES, LANES, LANES), F32),
            pltpu.VMEM((2, n, LANES), F32),
            pltpu.VMEM((LANES, LANES), F32),
            pltpu.VMEM((2, own, n), BF16),
            dma((2, CHUNKS)), dma((2, CHUNKS)),
            dma((14,)), dma((14,)),
            dma((PANELS * SPLITS, 10)), dma((PANELS * SPLITS, 10)),
            dma((PANELS * SPLITS, 27)), dma((PANELS * SPLITS, 27)),
            dma((4,)),
        ],
        compiler_params=pltpu.CompilerParams(
            collective_id=0, has_side_effects=True, vmem_limit_bytes=58 * 2**20
        ),
    )(lf, feats, wts)


def per_device(features, left_factor, ard_weights):
    lf = left_factor.reshape(4, BLOCK, 2, -1)
    feats = features.reshape(4, SHARE, -1)
    panels = panels_of(lf, feats, ard_weights.reshape(1, -1))
    return panels.reshape(4, 1, 1, SHARE, PANELS * BLOCK)


def solution(mesh):
    return jax.shard_map(
        per_device,
        mesh=mesh,
        in_specs=(P(None, "row", "col", None, None), P(None, "row", None, None, "col", None), P()),
        out_specs=P(None, "row", "col", None, None),
        check_vma=False,
    )
```

time: 1200 us -> 187 us (0.16)
  waiting for transfers between devices: 772 us -> 0 us
  other arithmetic: 254 us -> 0 us
  Pallas kernels: 0 us -> 184 us
  blocking collectives: 52.5 us -> 0 us
  local copies, waits for them, and re-layouts: 51.4 us -> 1.67 us
  matrix products: 38.6 us -> 0 us
  between operations: 19.3 us -> 0.01 us
    reduce_scatter x2 -> x0, waiting for transfers between devices: 432 us -> none  [panel_update(): lax.psum_scatter(make_term(local_view, factor_rows, rows_here, rows_here...]
    another operation x34 -> x0, other arithmetic: 243 us -> none  [the longest x29 163 us: inverse_factor(): factor = jnp.linalg.cholesky(matrix)]
    psum x3 -> x0, waiting for transfers between devices: 192 us -> none  [from_root(): return lax.psum(jnp.where(mine, x, jnp.zeros_like(x)), axis)]
    pallas_call x0 -> x1, Pallas kernels: none -> 184 us  [panels_of(): pl.pallas_call(panels_kernel, out_shape=jax.ShapeDtypeStruct((own, n), F3...]
    all_gather x2 -> x0, waiting for transfers between devices: 147 us -> none  [the longest x1 74.2 us: per_device(): lax.all_gather(first_schur[:share_rows], 'col', axis=0, tiled=True)]
    all_gather x1 -> x0, blocking collectives: 52.5 us -> none  [per_device(): block_feats = lax.all_gather(features[0, 0, 0], 'col', axis=0, tiled=True)]
    dot_general x8 -> x0, matrix products: 25 us -> none  [the longest x6 12.9 us: contract_rows(): lax.dot_general(left_mat, right_mat, (((1,), (1,)), ((), ())), precision=...]
    another operation x35 -> x0, local copies, waits for them, and re-layouts: 20.5 us -> none  [the longest x27 19.2 us: inverse_factor(): return jax.scipy.linalg.solve_triangular(factor, identity_mat, lower=True)]
  transfers between devices with their start and end apart: 7 -> 0, of which waited for: 7 -> 0; matrix products, arithmetic and copies ran while one was open for 2% -> 0% of each run, Pallas kernels for 0% -> 0%
where the time goes in v2:
time: 187 us; the launch traced here: 186 us
  Pallas kernels  184 us (98%)
    pallas_call x1, Pallas kernels, panels_of(): pl.pallas_call(panels_kernel, out_shape=jax.ShapeDtypeStruct((own, n), F3...  184 us

profile of v2, /device:TPU:24, one launch (start us, length us, event | category | flops | bytes accessed | tf_op | source)
XLA Modules:
  0.0 185.6 jit_solution(1735990386243815773)
XLA Ops:
  0.0 183.9 %shard_map.37 = f32[64,1024]{1,0:T(8,128)} custom-call(bf16[4,512,2,512]{3,2,1,0:T(2,128)(2,1)} %bitcast.6, bf16[4,16,512]{2,1,0:T(8,128)(2,1)} %bitcast.8, f32[1,512]{1,0:T(1,128)} %bitcast.9), custom_call_target="tpu_custom_call" | custom-call | tf_op jit(solution)/shard_map/pallas_call | solution.py:660
  183.9 1.7 copy.6

commit v3 on v2

--- a/solution.py
+++ b/solution.py
@@ -53,17 +53,17 @@
             recip = 1.0 / pivot
             scale = jnp.where(rows == j, lax.rsqrt(pivot), scale)
             cj = c[j]
+            both = jnp.where(rows == j, -1.0, cj)
             below = jnp.where(rows > j, cj, 0.0)
 
             def step(tile):
-                unit = sub_row(tile, j) * recip
-                return jnp.where(rows == j, unit, tile - cj * unit)
+                return jnp.where(rows == j, 0.0, tile) - (both * sub_row(tile, j)) * recip
 
             for k in range(j + 1, 8):
                 c[k] = step(c[k])
             if g < tiles - 1:
                 ta, tb = step(ta), step(tb)
-            tf = tf - below * (sub_row(tf, j) * recip)
+            tf = tf - (below * sub_row(tf, j)) * recip
         store_tile(g, tf * scale)
         if g < tiles - 1:
             wa = [sub_row(ta, j) for j in range(8)]
@@ -95,7 +95,7 @@
 def panels_kernel(
     lf_in, feats, wts, out_ref,
     raw, rt, lf, pan, fp, t, kern, bz1, bx1, bx2, bz2, rx, rz, sa, own_s,
-    lo, xs, col_buf, dg, po,
+    lo, xs, col_buf, dg, dacc, po,
     pan_s, pan_r, ft_s, ft_r, rs_s, rs_r, dg_s, dg_r, loc,
 ):
     row, col = lax.axis_index("row"), lax.axis_index("col")
@@ -273,18 +273,20 @@
 
         return (lambda: begin(order[0])), macro, drain
 
-    def rs_hop(g):
+    def rs_hop(g, kind):
         def go(rnd):
-            for h in range(SPLITS):
-                for b in range(PANELS):
+            for b in (core, 1 - core):
+                for h in range(kind, SPLITS, 2):
                     stream(b, h, rnd)[1](g)
 
         pl.when(off_y0)(lambda: go(0))
         pl.when(at_y0)(lambda: go(1))
 
-    def product(b, h, i):
-        rows = nt(lf[i], pan[b, h * LANES : (h + 1) * LANES, :], None)
-        t[b * SPLITS + h, :, i] = rows.reshape(NZ, NX, SHARE, LANES)
+    def product(b, pair, i):
+        rows = nt(lf[i], pan[b, pair * 2 * LANES : (pair + 1) * 2 * LANES, :], None)
+        for u in range(2):
+            q = b * SPLITS + pair * 2 + u
+            t[q, :, i] = rows[:, u * LANES : (u + 1) * LANES].reshape(NZ, NX, SHARE, LANES)
 
     def lanes_of(j):
         return pl.ds(j * LANES, LANES)
@@ -420,50 +422,68 @@
 
     lo[...] = jnp.zeros(lo.shape, BF16)
     po[...] = jnp.zeros(po.shape, BF16)
+    xs[7] = jnp.zeros((LANES, LANES), F32)
+    dacc[...] = jnp.zeros((LANES, LANES), F32)
+    col_buf[1] = jnp.zeros((n_cols, LANES), F32)
     sa[0, :, :, :, pl.ds(BLOCK, BLOCK)] = jnp.zeros((NZ, NX, SHARE, BLOCK), F32)
     for copy in raw_copies[1:]:
         copy.wait()
 
+    def begin(b, hs, rnd):
+        for h in hs:
+            stream(b, h, rnd)[0]()
+
     @pl.when(at_y0)
     def _():
-        for h in range(SPLITS):
-            sib_chunk(2 * h, 1 - core).wait_recv()
-            sib_chunk(2 * h + 1, 1 - core).wait_recv()
-            product(0, h, 0)
-            rsx_start(h)
-        f_x_start()
+        for pair in range(2):
+            for c in range(4 * pair, 4 * pair + 4):
+                sib_chunk(c, 1 - core).wait_recv()
+            product(0, pair, 0)
+            rsx_start(2 * pair)
+            rsx_start(2 * pair + 1)
         relayout_blocks(1)
 
         def rest(b):
             def go(i, carry):
-                for h in range(SPLITS):
-                    product(b, h, i)
+                product(b, 0, i)
+                product(b, 1, i)
                 return carry
 
             lax.fori_loop(1, 4, go, 0)
-            for h in range(SPLITS):
-                stream(b, h, 1)[0]()
 
         rest(0)
+        begin(0, (0, 2), 1)
+        f_x_start()
+        product(1, 0, 0)
+        product(1, 1, 0)
         for j in range(SPLITS):
             rsx_done(j)
+        for j in range(SPLITS, 2 * SPLITS):
+            rsx_start(j)
+        rest(1)
+        begin(1, (0, 2), 1)
         f_sib_start()
-        for h in range(SPLITS):
-            product(1, h, 0)
-            rsx_start(SPLITS + h)
         f_sib(1 - core).wait_recv()
         own_kernel()
         for j in range(SPLITS):
             rsz_done(j)
-        rest(1)
-        for j in range(SPLITS, 2 * SPLITS):
-            rsx_done(j)
+        begin(0, (1, 3), 1)
+        begin(1, (1, 3), 1)
 
     @pl.when(off_y0)
     def _():
         relayout_blocks(0)
         f_y(1).wait_recv()
         f_z_start()
+
+        def whole(b, pair):
+            def go(i, carry):
+                product(b, pair, i)
+                return carry
+
+            lax.fori_loop(0, 4, go, 0)
+            begin(b, (2 * pair, 2 * pair + 1), 0)
+
         for c in range(CHUNKS):
             ring_chunk(c).wait_recv()
 
@@ -472,19 +492,15 @@
                 ring_chunk(c).start()
 
             sib_chunk(c, core).start()
-            sib_chunk(c, 1 - core).wait_recv()
             if c == 3:
+                whole(core, 0)
                 f_x_start()
-            if c % 2 == 1:
-                def go(i, carry):
-                    product(0, c // 2, i)
-                    product(1, c // 2, i)
-                    return carry
-
-                lax.fori_loop(0, 4, go, 0)
-                for b in range(PANELS):
-                    stream(b, c // 2, 0)[0]()
+        whole(core, 1)
         f_sib_start()
+        for pair in range(2):
+            for c in range(4 * pair, 4 * pair + 4):
+                sib_chunk(c, 1 - core).wait_recv()
+            whole(1 - core, pair)
         f_sib(1 - core).wait_recv()
         own_kernel()
         for j in range(SPLITS):
@@ -499,23 +515,22 @@
     def block_of(value):
         return lambda v: value[8 * v : 8 * v + 8, :]
 
-    def rest_of(b):
-        off = pl.multiple_of(b * LANES, LANES)
-        noff = pl.multiple_of(off + LANES, LANES)
-        for i, half in enumerate(halves(nt(col_buf[lax.rem(b, 2)], xs[b]))):
-            lo[i, :, pl.ds(off, LANES)] = half
-        update = nt_halves((lo[0], lo[1]), (lo[0, pl.ds(noff, LANES), :], lo[1, pl.ds(noff, LANES), :]))
-        col_buf[lax.rem(b + 1, 2)] = sa[:, :, :, :, pl.ds(noff, LANES)].reshape(n_cols, LANES) - update
-
-    def next_diag(b):
-        off = pl.multiple_of(b * LANES, LANES)
-        noff = pl.multiple_of(off + LANES, LANES)
-        below = halves(nt(col_buf[lax.rem(b, 2), pl.ds(noff, LANES), :], xs[b]))
-        b1 = b + 1
-        block = sa[b1 // SPLITS, pl.ds(2 * lax.rem(b1, SPLITS), 2), :, :, pl.ds(noff, LANES)]
-        done = (lo[0, pl.ds(noff, LANES), :], lo[1, pl.ds(noff, LANES), :])
-        dg[...] = block.reshape(LANES, LANES) - nt_halves(done, done) - nt_halves(below, below)
-        diag_inverse(block_of(dg[...]), store_inverse(b1))
+    def step(b):
+        prev, after = lax.rem(b + 7, 8), lax.rem(b + 1, 8)
+        here = pl.ds(pl.multiple_of(b * LANES, LANES), LANES)
+        back = pl.ds(pl.multiple_of(prev * LANES, LANES), LANES)
+        ahead = pl.ds(pl.multiple_of(after * LANES, LANES), LANES)
+        last = col_buf.at[lax.rem(b + 1, 2)]
+        corner = halves(nt(last[here, :], xs[prev]))
+        block = sa[b // SPLITS, pl.ds(2 * lax.rem(b, SPLITS), 2), :, :, here]
+        dg[...] = block.reshape(LANES, LANES) - dacc[...] - nt_halves(corner, corner)
+        diag_inverse(block_of(dg[...]), store_inverse(b))
+        for i, half in enumerate(halves(nt(last[...], xs[prev]))):
+            lo[i, :, back] = half
+        update = nt_halves((lo[0], lo[1]), (lo[0, here, :], lo[1, here, :]))
+        col_buf[lax.rem(b, 2)] = sa[:, :, :, :, here].reshape(n_cols, LANES) - update
+        below = (lo[0, ahead, :], lo[1, ahead, :])
+        dacc[...] = nt_halves(below, below)
 
     def own_rows(b):
         lanes = pl.ds(pl.multiple_of(b * LANES, LANES), LANES)
@@ -526,65 +541,78 @@
             po[i, :, lanes] = half
 
     second = range(SPLITS, 2 * SPLITS)
+    rs_hop(0, 0)
     agz_done(0)
     agz_done(1)
     agx_done(0)
     agz_done(2)
     agx_done(1)
     sib_done(0)
-    col_buf[0] = sa[:, :, :, :, pl.ds(0, LANES)].reshape(n_cols, LANES)
-    diag_inverse(block_of(col_buf[0, 0:LANES, :]), store_inverse(0))
 
     def before_0():
         @pl.when(at_y0)
         def _():
             for j in second:
-                rsz_done(j)
-
+                rsx_done(j)
+
+        rs_hop(1, 0)
+
+    def before_1():
         agz_done(3)
         agx_done(2)
         sib_done(1)
 
-    def before_1():
+        @pl.when(at_y0)
+        def _():
+            for j in second:
+                rsz_done(j)
+
+        rs_hop(0, 1)
+
+    def before_2():
+        agx_done(3)
+        sib_done(2)
+
         @pl.when(off_y0)
         def _():
             for j in second:
                 agy_done(j)
 
-        agx_done(3)
-        sib_done(2)
-        rs_hop(0)
-
-    def before_2():
+        rs_hop(2, 0)
+
+    def before_3():
+        sib_done(3)
         for j in second:
             agz_done(j)
-        sib_done(3)
-        rs_hop(1)
-
-    def before_3():
+        rs_hop(1, 1)
+
+    def before_4():
         for j in second:
             agx_done(j)
         sib_done(4)
-        rs_hop(2)
-
-    def before_4():
+        rs_hop(3, 0)
+        rs_hop(2, 1)
+
+    def before_5():
         sib_done(5)
-        rs_hop(3)
-
-    def before_5():
+        rs_hop(4, 0)
+        rs_hop(3, 1)
+
+    def before_6():
         sib_done(6)
-        rs_hop(4)
-
-    def step(b, carry):
-        for k, fn in enumerate((before_0, before_1, before_2, before_3, before_4, before_5)):
+        rs_hop(5, 0)
+        rs_hop(4, 1)
+
+    def round_of(b, carry):
+        before = (before_0, before_1, before_2, before_3, before_4, before_5, before_6)
+        for k, fn in enumerate(before):
             pl.when(b == k)(fn)
-        next_diag(b)
-        rest_of(b)
+        step(b)
         return carry
 
-    lax.fori_loop(0, 6, step, 0)
+    lax.fori_loop(0, 7, round_of, 0)
     sib_done(7)
-    rs_hop(5)
+    rs_hop(5, 1)
 
     def own_schur(i):
         for q in range(PANELS * SPLITS):
@@ -594,8 +622,7 @@
     pl.when(off_y0)(lambda: own_schur(0))
     for i in range(1, 4):
         own_schur(i)
-    next_diag(6)
-    rest_of(6)
+    step(7)
     for b in range(8):
         own_rows(b)
 
@@ -682,6 +709,7 @@
             pltpu.VMEM((n // LANES, LANES, LANES), F32),
             pltpu.VMEM((2, n, LANES), F32),
             pltpu.VMEM((LANES, LANES), F32),
+            pltpu.VMEM((LANES, LANES), F32),
             pltpu.VMEM((2, own, n), BF16),
             dma((2, CHUNKS)), dma((2, CHUNKS)),
             dma((14,)), dma((14,)),

time: 187 us -> 147 us (0.79)
  Pallas kernels: 184 us -> 143 us
    pallas_call x1, Pallas kernels: 184 us -> 143 us  [panels_of(): pl.pallas_call(panels_kernel, out_shape=jax.ShapeDtypeStruct((own, n), F3...]
where the time goes in v3:
time: 147 us; the launch traced here: 145 us
  Pallas kernels  143 us (97%)
  local copies, waits for them, and re-layouts  1.67 us (1%)
    pallas_call x1, Pallas kernels, panels_of(): pl.pallas_call(panels_kernel, out_shape=jax.ShapeDtypeStruct((own, n), F3...  143 us

profile of v3, /device:TPU:24, one launch (start us, length us, event | category | flops | bytes accessed | tf_op | source)
XLA Modules:
  0.0 145.1 jit_solution(11404937049655576246)
XLA Ops:
  0.0 143.4 %shard_map.37 = f32[64,1024]{1,0:T(8,128)} custom-call(bf16[4,512,2,512]{3,2,1,0:T(2,128)(2,1)} %bitcast.6, bf16[4,16,512]{2,1,0:T(8,128)(2,1)} %bitcast.8, f32[1,512]{1,0:T(1,128)} %bitcast.9), custom_call_target="tpu_custom_call" | custom-call | tf_op jit(solution)/shard_map/pallas_call | solution.py:687
  143.4 1.7 %copy.6 = f32[4,1,1,16,1024]{4,3,2,1,0:T(8,128)} copy(f32[4,1,1,16,1024]{4,3,2,1,0:T(8,128)} %bitcast.7) | data formatting | bytes 524288

commit v4 on v3

--- a/solution.py
+++ b/solution.py
@@ -46,10 +46,11 @@
     e = [jnp.where(lanes == rows + 8 * v, 1.0, 0.0).astype(F32) for v in range(tiles)]
     for g in range(tiles):
         c = [lane_col(a[g], 8 * g + j) for j in range(8)]
+        pivots = [sub_row(c[k], k) for k in range(8)]
         ta, tb, tf = a[g], e[g], e[g]
         scale = jnp.zeros((8, LANES), F32)
         for j in range(8):
-            pivot = sub_row(c[j], j)
+            pivot = pivots[j]
             recip = 1.0 / pivot
             scale = jnp.where(rows == j, lax.rsqrt(pivot), scale)
             cj = c[j]
@@ -60,7 +61,9 @@
                 return jnp.where(rows == j, 0.0, tile) - (both * sub_row(tile, j)) * recip
 
             for k in range(j + 1, 8):
-                c[k] = step(c[k])
+                unit = sub_row(c[k], j)
+                pivots[k] = pivots[k] - (unit * unit) * recip
+                c[k] = jnp.where(rows == j, 0.0, c[k]) - (both * unit) * recip
             if g < tiles - 1:
                 ta, tb = step(ta), step(tb)
             tf = tf - (below * sub_row(tf, j)) * recip
@@ -461,14 +464,13 @@
         for j in range(SPLITS, 2 * SPLITS):
             rsx_start(j)
         rest(1)
-        begin(1, (0, 2), 1)
         f_sib_start()
+        begin(0, (1, 3), 1)
+        begin(1, range(SPLITS), 1)
         f_sib(1 - core).wait_recv()
         own_kernel()
         for j in range(SPLITS):
             rsz_done(j)
-        begin(0, (1, 3), 1)
-        begin(1, (1, 3), 1)
 
     @pl.when(off_y0)
     def _():

time: 147 us -> 145 us (0.986)
  no operation moved by 1% of the time
where the time goes in v4:
time: 145 us; the launch traced here: 144 us
  Pallas kernels  142 us (98%)
  local copies, waits for them, and re-layouts  1.67 us (1%)
    pallas_call x1, Pallas kernels, panels_of(): pl.pallas_call(panels_kernel, out_shape=jax.ShapeDtypeStruct((own, n), F3...  142 us

profile of v4, /device:TPU:24, one launch (start us, length us, event | category | flops | bytes accessed | tf_op | source)
XLA Modules:
  0.0 143.9 jit_solution(9490127017190414109)
XLA Ops:
  0.0 142.2 %shard_map.37 = f32[64,1024]{1,0:T(8,128)} custom-call(bf16[4,512,2,512]{3,2,1,0:T(2,128)(2,1)} %bitcast.6, bf16[4,16,512]{2,1,0:T(8,128)(2,1)} %bitcast.8, f32[1,512]{1,0:T(1,128)} %bitcast.9), custom_call_target="tpu_custom_call" | custom-call | tf_op jit(solution)/shard_map/pallas_call | solution.py:689
  142.2 1.7 %copy.6 = f32[4,1,1,16,1024]{4,3,2,1,0:T(8,128)} copy(f32[4,1,1,16,1024]{4,3,2,1,0:T(8,128)} %bitcast.7) | data formatting | bytes 524288
